TPU v7x, 128 devices: a whole 4x4x4 slice. The times are simulated.
128 devices in a mesh: dp: 64 (over z, y, x), ctx: 2 (over core).
Axes of the slice: x: 4, y: 4, z: 4, core: 2. Of those that a mesh axis runs over, the one named last changes fastest.
Arguments:
- queries: bfloat16 [64, 512, 4096], P('dp', 'ctx'), may hold values from -8 to 8
- keys: bfloat16 [64, 512, 512], P('dp', 'ctx'), may hold values from -8 to 8
- values: bfloat16 [64, 512, 512], P('dp', 'ctx'), may hold values from -6 to 6
- out_grad: bfloat16 [64, 512, 4096], P('dp', 'ctx'), may hold values from -6 to 6
- ssm_in: bfloat16 [64, 512, 8192], P('dp', 'ctx'), may hold values from -6 to 6
- ssm_b: bfloat16 [64, 512, 512], P('dp', 'ctx'), may hold values from -0.41992188 to 0.41992188
- ssm_c: bfloat16 [64, 512, 512], P('dp', 'ctx'), may hold values from -0.41992188 to 0.41992188
- step_size: bfloat16 [64, 512, 128], P('dp', 'ctx'), may hold values from 0.5 to 2
- y_grad: bfloat16 [64, 512, 8192], P('dp', 'ctx'), may hold values from -6 to 6
- a_log: float32 [128], replicated, may hold values from -8.5 to -3.5
- segments: int32 [64, 512], P('dp'), may hold values from 0 to 3, never falling along the last dimension, each value on 1 to 256 neighbouring positions
- plan: int32 [64, 64], replicated, may hold values from 0 to 63, as said below
Outputs:
- q_grad: bfloat16 [64, 512, 4096], P('dp', 'ctx')
- k_grad: bfloat16 [64, 512, 512], P('dp', 'ctx')
- v_grad: bfloat16 [64, 512, 512], P('dp', 'ctx')
- in_grad: bfloat16 [64, 512, 8192], P('dp', 'ctx')
- b_grad: bfloat16 [64, 512, 512], P('dp', 'ctx')
- c_grad: bfloat16 [64, 512, 512], P('dp', 'ctx')
- step_grad: float32 [64, 512, 128], P('dp', 'ctx')
- a_log_grad: float32 [128], replicated
Inputs may be any that keep to these rules, and one draw needn't show every extreme that they name: `plan`: block number g of stream i goes to stream (i + o_g) mod 64, the 64 offsets o_g a permutation of 0 to 63; so a stream sends exactly one block to each stream and receives exactly one from each, and the block that leaves as number g arrives as number g.
All inputs are finite; a program needn't handle non-finite values.
Results may differ from a plain program's by a relative error of at most 0.0093.
Values may be sent and summed in bfloat16 or wider, within the bound.
No kernel may reach another device: no remote copies, remote signals or barrier semaphores. Data moves between devices by JAX's collectives and lax.ppermute only.
A program may use at most 320 MiB of HBM per device.

v0:
```python
import functools

import jax
import jax.numpy as jnp
from jax import lax
from jax.experimental import pallas as pl
from jax.experimental.pallas import tpu as pltpu
from jax.sharding import PartitionSpec as P

KV_HEADS = 4
GROUP_HEADS = 8
DEPTH = 128
MH = 128
MP = 64
MN = 128
MG = 4
TOK = 256
WINDOW = 288
PIECE = 8
HALVES = 2
BLK = 4
STRIDE = 7
ORDER = [(STRIDE * p) % 64 for p in range(64)]
PLACE_OF = [ORDER.index(d) for d in range(64)]
QROWS = 32
TOGETHER = 8
QW = GROUP_HEADS * DEPTH
XW = (MH // MG) * MP
SCALE = DEPTH ** -0.5
LOG2E = 1.4426950408889634
MASKED = -1e30
VMEM_LIMIT = 56 * 1024 * 1024

F32 = jnp.float32
BF16 = jnp.bfloat16


def nn(a, b):
    return lax.dot_general(a, b, (((1,), (0,)), ((), ())), preferred_element_type=F32)


def nt(a, b):
    return lax.dot_general(a, b, (((1,), (1,)), ((), ())), preferred_element_type=F32)


def split_two(values):
    high = values.astype(BF16)
    return high, (values - high.astype(F32)).astype(BF16)


def params(count=0):
    if count:
        return pltpu.CompilerParams(
            vmem_limit_bytes=VMEM_LIMIT, dimension_semantics=("arbitrary",) * count
        )
    return pltpu.CompilerParams(vmem_limit_bytes=VMEM_LIMIT)


def cost(flops, nbytes):
    return pl.CostEstimate(flops=int(flops), bytes_accessed=int(nbytes), transcendentals=0)


def pack_plan(parts):
    jobs, at = [], 0
    for array, first, half, both in parts:
        step = min(half, 1024)
        for k in range(0, half, step):
            jobs.append((array, first + k, first + half + k, step, both, at))
            at += step
    return jobs, at


def pack_kernel(jobs, narrays, *refs):
    select_ref, arrays, out_ref = refs[0], refs[1 : 1 + narrays], refs[1 + narrays]
    stack, packed, in_sems, out_sems = refs[2 + narrays :]
    loads = []
    for j, (array, low, high, step, both, at) in enumerate(jobs):
        pair = []
        for w, first in enumerate((low, high) if both else (low,)):
            copy = pltpu.make_async_copy(
                arrays[array].at[:, pl.ds(first, step)],
                stack.at[w, :, pl.ds(at, step)],
                in_sems.at[j, w],
            )
            copy.start()
            pair.append(copy)
        loads.append(pair)
    plain, swapped = select_ref[0], select_ref[1]
    pairs = packed.shape[0]
    stores = []
    for j, (array, low, high, step, both, at) in enumerate(jobs):
        for copy in loads[j]:
            copy.wait()
        one = nn(plain, stack[0, :, at : at + step]).reshape(pairs, PIECE, step)
        if both:
            two = nn(swapped, stack[1, :, at : at + step]).reshape(pairs, PIECE, step)
            upper = lax.broadcasted_iota(jnp.int32, (pairs, PIECE, step), 1) < BLK
            even, odd = jnp.where(upper, one, two), jnp.where(upper, two, one)
        else:
            even = odd = one
        packed[:, :, at : at + step] = jnp.concatenate([even, odd], axis=1).astype(BF16)
        copy = pltpu.make_async_copy(
            packed.at[:, :, pl.ds(at, step)], out_ref.at[:, :, pl.ds(at, step)], out_sems.at[j]
        )
        copy.start()
        stores.append(copy)
    for copy in stores:
        copy.wait()


def pack(select, arrays, parts, spare=0):
    jobs, filled = pack_plan(parts)
    width = filled + spare
    pairs = TOK // PIECE
    return pl.pallas_call(
        functools.partial(pack_kernel, jobs, len(arrays)),
        out_shape=jax.ShapeDtypeStruct((pairs, 2 * PIECE, width), BF16),
        in_specs=[pl.BlockSpec(memory_space=pltpu.VMEM)]
        + [pl.BlockSpec(memory_space=pltpu.HBM)] * len(arrays),
        out_specs=pl.BlockSpec(memory_space=pl.ANY),
        scratch_shapes=[
            pltpu.VMEM((2, TOK, width), BF16),
            pltpu.VMEM((pairs, 2 * PIECE, width), BF16),
            pltpu.SemaphoreType.DMA((len(jobs), 2)),
            pltpu.SemaphoreType.DMA((len(jobs),)),
        ],
        compiler_params=params(),
        cost_estimate=cost(4 * TOK * TOK * width, 8 * TOK * width),
        name="pack",
    )(select, *arrays)


def exchange(packed):
    pairs, _, width = packed.shape
    pieces = packed.reshape(2 * pairs, PIECE, width)
    moved = lax.all_to_all(pieces, "dp", split_axis=0, concat_axis=0, tiled=True, axis_index_groups=[ORDER])
    return moved.reshape(2 * pairs * PIECE, width)


def small_kernel(r_ref, step_ref, place_ref, alog_ref, same_ref, flag_ref, kv_ref, bc_ref, dt_ref, e_ref, f_ref, col_ref):
    place = place_ref[...]
    first, second = place[:TOK], place[TOK:]
    for n, (out, at) in enumerate(((kv_ref, 0), (kv_ref, 512), (bc_ref, 0), (bc_ref, 512))):
        part = r_ref[:, 256 * n : 256 * (n + 1)]
        out[:, at : at + 256] = nn(first, part).astype(BF16)
        out[:, at + 256 : at + 512] = nn(second, part).astype(BF16)
    steps_low = nn(first, step_ref[...]).astype(BF16)
    steps = steps_low.astype(F32)
    dt_ref[...] = steps
    t_at = lax.broadcasted_iota(jnp.int32, (TOK, TOK), 0)
    s_at = lax.broadcasted_iota(jnp.int32, (TOK, TOK), 1)
    lower = jnp.where(t_at >= s_at, 1.0, 0.0).astype(BF16)
    cumulative = -nn(lower, steps_low) * jnp.exp(alog_ref[...])
    e_high, e_low = split_two(jnp.exp(cumulative))
    f_high, f_low = split_two(steps * jnp.exp(-cumulative))
    e_ref[:, :128] = e_high
    e_ref[:, 128:] = e_low
    f_ref[:, :128] = f_high
    f_ref[:, 128:] = f_low
    first_core = flag_ref[0] > 0.5
    same = same_ref[...]
    for g in range(MG):
        b_one = bc_ref[:, 128 * g : 128 * (g + 1)].astype(F32)
        c_one = bc_ref[:, 512 + 128 * g : 512 + 128 * (g + 1)].astype(F32)
        col_ref[:, 128 * g : 128 * (g + 1)] = (jnp.where(first_core, b_one, c_one) * same).astype(BF16)


def small(received, place, a_log, same, flag):
    vmem = pl.BlockSpec(memory_space=pltpu.VMEM)
    return pl.pallas_call(
        small_kernel,
        grid=(1,),
        out_shape=(
            jax.ShapeDtypeStruct((TOK, 1024), BF16),
            jax.ShapeDtypeStruct((TOK, 1024), BF16),
            jax.ShapeDtypeStruct((TOK, MH), F32),
            jax.ShapeDtypeStruct((TOK, 256), BF16),
            jax.ShapeDtypeStruct((TOK, 256), BF16),
            jax.ShapeDtypeStruct((TOK, 512), BF16),
        ),
        in_specs=[
            pl.BlockSpec((received.shape[0], 1024), lambda i: (0, 4)),
            pl.BlockSpec((received.shape[0], 128), lambda i: (0, 40)),
            vmem,
            vmem,
            vmem,
            pl.BlockSpec(memory_space=pltpu.SMEM),
        ],
        out_specs=(vmem,) * 6,
        compiler_params=params(1),
        cost_estimate=cost(2 * 512 * 512 * 1152, 4e6),
        name="small",
    )(received, received, place, a_log, same, flag)


def attention_kernel(split, *refs):
    (qr_ref, or_ref, place_ref, ko_ref, vo_ref, kp_ref, vp_ref, bias_ref) = refs[:8]
    dq_ref, own_ref, before_ref = refs[-6:-3]
    qo, dk, dv = refs[-3:]
    for n in range(2):
        lanes = slice(512 * n, 512 * (n + 1))
        place = place_ref[TOK * n : TOK * (n + 1)] if split else place_ref[...]
        taken = slice(None) if split else lanes
        qo[:, lanes] = nn(place, qr_ref[:, taken]).astype(BF16)
        qo[:, QW + 512 * n : QW + 512 * (n + 1)] = nn(place, or_ref[:, taken]).astype(BF16)
    k_cat = jnp.concatenate([kp_ref[...], ko_ref[...]], axis=0)
    v_cat = jnp.concatenate([vp_ref[...], vo_ref[...]], axis=0)
    dk[...] = jnp.zeros_like(dk)
    dv[...] = jnp.zeros_like(dv)
    turns = [(i, r) for i in range(TOK // QROWS) for r in range(0, GROUP_HEADS, TOGETHER)]

    def products(i, r):
        rows = slice(QROWS * i, QROWS * (i + 1))
        keys = slice(QROWS * i, QROWS * i + WINDOW)
        heads = [DEPTH * (r + n) for n in range(TOGETHER)]
        q_some = jnp.concatenate([qo[rows, h : h + DEPTH] for h in heads], axis=0)
        o_some = jnp.concatenate([qo[rows, QW + h : QW + h + DEPTH] for h in heads], axis=0)
        return rows, keys, heads, q_some, o_some, nt(k_cat[keys], q_some), nt(v_cat[keys], o_some)

    def finish_turn(rows, keys, heads, q_some, o_some, weights_low, score_grad):
        dv[keys, :] += nn(weights_low, o_some)
        dk[keys, :] += nn(score_grad, q_some)
        dq_some = (nn(k_cat[keys].T, score_grad) * SCALE).T.astype(BF16)
        for n, h in enumerate(heads):
            dq_ref[rows, h : h + DEPTH] = dq_some[QROWS * n : QROWS * (n + 1)]

    ahead, behind = products(*turns[0]), None
    for at, (i, _) in enumerate(turns):
        *places, scores, pulled = ahead
        if at + 1 < len(turns):
            ahead = products(*turns[at + 1])
        bias = bias_ref[i]
        bias = jnp.concatenate([bias, bias], axis=1)
        scores = scores * (SCALE * LOG2E) + bias
        raised = jnp.exp2(scores - jnp.max(scores, axis=0, keepdims=True))
        weights = raised * (1.0 / jnp.sum(raised, axis=0, keepdims=True))
        delta = jnp.sum(weights * pulled, axis=0, keepdims=True)
        score_grad = (weights * (pulled - delta)).astype(BF16)
        if behind is not None:
            finish_turn(*behind)
        behind = (*places, weights.astype(BF16), score_grad)
    finish_turn(*behind)
    before_ref[0] = (dk[:TOK] * SCALE).astype(BF16)
    before_ref[1] = dv[:TOK].astype(BF16)
    own_ref[0] = (dk[TOK:] * SCALE).astype(BF16)
    own_ref[1] = dv[TOK:].astype(BF16)


def attention(received, block, first_group, groups, place, kv_own, kv_before, bias, dq_before):
    split = groups == 1
    width, rows = (QW // 2, 2 * TOK) if split else (QW, TOK)
    key_at = lambda g: (0, first_group + g)
    value_at = lambda g: (0, KV_HEADS + first_group + g)
    in_specs = [
        pl.BlockSpec((received.shape[0], width), lambda g: (0, block)),
        pl.BlockSpec((received.shape[0], width), lambda g: (0, block + 1)),
        pl.BlockSpec((rows, place.shape[1]), lambda g: (g, 0)),
        pl.BlockSpec((TOK, DEPTH), key_at),
        pl.BlockSpec((TOK, DEPTH), value_at),
        pl.BlockSpec((TOK, DEPTH), key_at),
        pl.BlockSpec((TOK, DEPTH), value_at),
        pl.BlockSpec(bias.shape, lambda g: (0, 0, 0)),
    ]
    operands = [received, received, place, kv_own, kv_own, kv_before, kv_before, bias]
    aliases = {}
    if dq_before is not None:
        in_specs.append(pl.BlockSpec(memory_space=pl.ANY))
        operands.append(dq_before)
        aliases = {8: 0}
    return pl.pallas_call(
        functools.partial(attention_kernel, split),
        grid=(groups,),
        out_shape=(
            jax.ShapeDtypeStruct((TOK, KV_HEADS * QW), BF16),
            jax.ShapeDtypeStruct((2, TOK, groups * DEPTH), BF16),
            jax.ShapeDtypeStruct((2, TOK, groups * DEPTH), BF16),
        ),
        in_specs=in_specs,
        out_specs=(
            pl.BlockSpec((TOK, QW), lambda g: (0, first_group + g)),
            pl.BlockSpec((2, TOK, DEPTH), lambda g: (0, 0, g)),
            pl.BlockSpec((2, TOK, DEPTH), lambda g: (0, 0, g)),
        ),
        scratch_shapes=[
            pltpu.VMEM((TOK, 2 * QW), BF16),
            pltpu.VMEM((2 * TOK, DEPTH), F32),
            pltpu.VMEM((2 * TOK, DEPTH), F32),
        ],
        input_output_aliases=aliases,
        compiler_params=params(1),
        cost_estimate=cost(groups * 6e9, groups * 4e6),
        name="attention",
    )(*operands)


def state_kernel(xr_ref, dyr_ref, place_ref, e_ref, f_ref, col_ref, spread, flag_ref, x_ref, dy_ref, state_ref):
    place = place_ref[...]
    first_core = flag_ref[0] > 0.5
    col_turned = col_ref[...].astype(F32).T.astype(BF16)
    step = 512
    for at in range(0, XW, step):
        lanes = slice(at, at + step)
        e_wide = nn(e_ref[...], spread[:, lanes])
        f_wide = nn(f_ref[...], spread[:, lanes])
        x_low = (nn(place, xr_ref[:, lanes]) * f_wide).astype(BF16)
        dy_low = (nn(place, dyr_ref[:, lanes]) * e_wide).astype(BF16)
        x_ref[:, lanes] = x_low
        dy_ref[:, lanes] = dy_low
        sent = jnp.where(first_core, x_low, dy_low)
        gain = jnp.where(first_core, e_wide[TOK - 1 : TOK, :], 1.0)
        state_ref[:, lanes] = (nn(col_turned, sent) * gain).astype(BF16)


def state(received, first_group, groups, place, e_two, f_two, columns, spread, flag):
    whole = lambda g: (0, 0)
    return pl.pallas_call(
        state_kernel,
        grid=(groups,),
        out_shape=(
            jax.ShapeDtypeStruct((TOK, groups * XW), BF16),
            jax.ShapeDtypeStruct((TOK, groups * XW), BF16),
            jax.ShapeDtypeStruct((MN, groups * XW), BF16),
        ),
        in_specs=[
            pl.BlockSpec((received.shape[0], XW), whole),
            pl.BlockSpec((received.shape[0], XW), lambda g: (0, 1)),
            pl.BlockSpec((TOK, place.shape[1]), lambda g: (g, 0)),
            pl.BlockSpec((TOK, 2 * MH), whole),
            pl.BlockSpec((TOK, 2 * MH), whole),
            pl.BlockSpec((TOK, MN), lambda g: (0, first_group + g)),
            pl.BlockSpec((2 * MH, XW), lambda g: (0, first_group + g)),
            pl.BlockSpec(memory_space=pltpu.SMEM),
        ],
        out_specs=(
            pl.BlockSpec((TOK, XW), lambda g: (0, g)),
            pl.BlockSpec((TOK, XW), lambda g: (0, g)),
            pl.BlockSpec((MN, XW), lambda g: (0, g)),
        ),
        compiler_params=params(1),
        cost_estimate=cost(groups * 3e9, 14e6),
        name="state",
    )(received, received, place, e_two, f_two, columns, spread, flag)


def scan_kernel(*refs):
    (x_ref, dy_ref, b_ref, c_ref, col_ref, state_ref, e_ref, f_ref) = refs[:8]
    (mask_ref, turned_ref, same_ref, spread, gather, flag_ref) = refs[8:14]
    dx_ref, db_ref, dc_ref, sums_ref = refs[-4:]
    step_at = pl.program_id(0)
    first = flag_ref[0]
    second = 1.0 - first
    first_core = first > 0.5
    b_one, c_one = b_ref[...], c_ref[...]
    mask, turned = mask_ref[...], turned_ref[...]
    cb = (nt(c_one, b_one) * mask).astype(BF16)
    bc = (nt(b_one, c_one) * turned).astype(BF16)
    col = col_ref[...]
    f_two = f_ref[...]
    e_last = e_ref[TOK - 16 : TOK, :]

    d_cb = jnp.zeros((TOK, TOK), F32)
    d_col = jnp.zeros((TOK, MN), F32)
    d_cum = jnp.zeros((TOK, MH), F32)
    own = jnp.zeros((TOK, MH), F32)
    last = jnp.zeros((8, MH), F32)
    step = 512
    for at in range(0, XW, step):
        lanes = slice(at, at + step)
        x_low, dy_low = x_ref[:, lanes], dy_ref[:, lanes]
        gain = jnp.where(first_core, nn(e_last, spread[:, lanes])[15:16, :], 1.0)
        state_low = (state_ref[:, lanes].astype(F32) * gain).astype(BF16)
        carried = nn(col, state_low)
        y = nn(cb, x_low) + carried * second
        u = nn(bc, dy_low) + carried * first
        f_wide = nn(f_two, spread[:, lanes])
        dx_ref[:, lanes] = (f_wide * u).astype(BF16)
        x_f = x_low.astype(F32)
        x_term = x_f * u
        both = dy_low.astype(F32) * y - x_term
        gather_one = gather[lanes, :]
        high, low = split_two(both)
        d_cum += nn(high, gather_one) + nn(low, gather_one)
        own += nn(x_term.astype(BF16), gather_one)
        tail = jnp.sum(x_f * carried, axis=0, keepdims=True) * first
        high, low = split_two(jnp.broadcast_to(tail, (8, step)))
        last += nn(high, gather_one) + nn(low, gather_one)
        d_cb += nt(dy_low, x_low)
        d_col += nt(jnp.where(first_core, x_low, dy_low), state_low)
    d_col = d_col * same_ref[...]
    dc_ref[...] = (nn((d_cb * mask).astype(BF16), b_one) + d_col * second).astype(BF16)
    db_ref[...] = (nn((d_cb * mask).T.astype(BF16), c_one) + d_col * first).astype(BF16)
    row = lax.broadcasted_iota(jnp.int32, (TOK, MH), 0)
    d_cum = d_cum + jnp.where(row == TOK - 1, last[0:1, :], 0.0)

    @pl.when(step_at == 0)
    def _():
        sums_ref[0] = d_cum
        sums_ref[1] = own

    @pl.when(step_at > 0)
    def _():
        sums_ref[0] += d_cum
        sums_ref[1] += own


def scan(x_low, dy_low, first_group, groups, bc, columns, states, e_two, f_two, mask, turned, same, spread, gather, flag, before):
    whole = lambda g: (0, 0)
    in_specs = [
        pl.BlockSpec((TOK, XW), lambda g: (0, g)),
        pl.BlockSpec((TOK, XW), lambda g: (0, g)),
        pl.BlockSpec((TOK, MN), lambda g: (0, first_group + g)),
        pl.BlockSpec((TOK, MN), lambda g: (0, MG + first_group + g)),
        pl.BlockSpec((TOK, MN), lambda g: (0, first_group + g)),
        pl.BlockSpec((MN, XW), lambda g: (0, g)),
        pl.BlockSpec((TOK, 2 * MH), whole),
        pl.BlockSpec((TOK, 2 * MH), whole),
        pl.BlockSpec((TOK, TOK), whole),
        pl.BlockSpec((TOK, TOK), whole),
        pl.BlockSpec((TOK, MN), whole),
        pl.BlockSpec((2 * MH, XW), lambda g: (0, first_group + g)),
        pl.BlockSpec((XW, MH), lambda g: (first_group + g, 0)),
        pl.BlockSpec(memory_space=pltpu.SMEM),
    ]
    operands = [x_low, dy_low, bc, bc, columns, states, e_two, f_two, mask, turned, same]
    operands += [spread, gather, flag]
    aliases = {}
    if before is not None:
        in_specs += [pl.BlockSpec(memory_space=pl.ANY)] * 3
        operands += list(before)
        aliases = {14: 0, 15: 1, 16: 2}
    return pl.pallas_call(
        scan_kernel,
        grid=(groups,),
        out_shape=(
            jax.ShapeDtypeStruct((TOK, MG * XW), BF16),
            jax.ShapeDtypeStruct((TOK, MG * MN), BF16),
            jax.ShapeDtypeStruct((TOK, MG * MN), BF16),
            jax.ShapeDtypeStruct((2, TOK, MH), F32),
        ),
        in_specs=in_specs,
        out_specs=(
            pl.BlockSpec((TOK, XW), lambda g: (0, first_group + g)),
            pl.BlockSpec((TOK, MN), lambda g: (0, first_group + g)),
            pl.BlockSpec((TOK, MN), lambda g: (0, first_group + g)),
            pl.BlockSpec((2, TOK, MH), lambda g: (0, 0, 0)),
        ),
        input_output_aliases=aliases,
        compiler_params=params(1),
        cost_estimate=cost(groups * 4e9, 10e6),
        name="scan",
    )(*operands)


def finish_kernel(one_ref, two_ref, dt_ref, alog_ref, step_ref, decay_ref):
    d_cum = one_ref[0] + two_ref[0]
    own = one_ref[1] + two_ref[1]
    t_at = lax.broadcasted_iota(jnp.int32, (TOK, TOK), 0)
    s_at = lax.broadcasted_iota(jnp.int32, (TOK, TOK), 1)
    upper = jnp.where(t_at <= s_at, 1.0, 0.0).astype(BF16)
    high, rest = split_two(d_cum)
    middle, low = split_two(d_cum - high.astype(F32))
    d_decay = nn(upper, high) + nn(upper, middle) + nn(upper, low)
    rate = jnp.exp(alog_ref[...])
    steps = dt_ref[...]
    step_ref[...] = own / steps - rate * d_decay
    decay_ref[...] = -rate * jnp.sum(steps * d_decay, axis=0, keepdims=True)


def finish(one, two, steps, a_log):
    return pl.pallas_call(
        finish_kernel,
        out_shape=(
            jax.ShapeDtypeStruct((TOK, MH), F32),
            jax.ShapeDtypeStruct((1, MH), F32),
        ),
        compiler_params=params(),
        cost_estimate=cost(1e8, 1e6),
        name="finish",
    )(one, two, steps, a_log)


def slot_kernel(values_ref, _, out_ref):
    high, rest = split_two(values_ref[...])
    middle, low = split_two(values_ref[...] - high.astype(F32))
    zeros = jnp.zeros((PIECE - 3, MH), F32)
    rows = [high.astype(F32), middle.astype(F32), low.astype(F32), zeros]
    piece = jnp.concatenate(rows + rows, axis=0).astype(BF16)
    out_ref[...] = jnp.broadcast_to(piece[None], out_ref.shape)


def fill_slot(values, packed):
    pairs, rows, width = packed.shape
    return pl.pallas_call(
        slot_kernel,
        grid=(1,),
        out_shape=jax.ShapeDtypeStruct(packed.shape, BF16),
        in_specs=[
            pl.BlockSpec((1, MH), lambda i: (0, 0)),
            pl.BlockSpec(memory_space=pl.ANY),
        ],
        out_specs=pl.BlockSpec((pairs, rows, MH), lambda i: (0, 0, width // MH - 1)),
        input_output_aliases={1: 0},
        compiler_params=params(1),
        cost_estimate=cost(1e6, 3e5),
        name="fill_slot",
    )(values, packed)


def sum_slots_kernel(slots_ref, out_ref):
    rows = slots_ref[...].astype(F32)
    row = lax.broadcasted_iota(jnp.int32, rows.shape, 0) % PIECE
    out_ref[...] = jnp.sum(jnp.where(row < 3, rows, 0.0), axis=0, keepdims=True)


def sum_slots(received):
    rows, width = received.shape
    return pl.pallas_call(
        sum_slots_kernel,
        grid=(1,),
        out_shape=jax.ShapeDtypeStruct((1, MH), F32),
        in_specs=[pl.BlockSpec((rows, MH), lambda i: (0, width // MH - 1))],
        out_specs=pl.BlockSpec((1, MH), lambda i: (0, 0)),
        compiler_params=params(1),
        cost_estimate=cost(1e5, 2e5),
        name="sum_slots",
    )(received)


def join_kernel(count, *refs):
    k_ref, v_ref = refs[-2:]
    at = 0
    for own, other in zip(refs[:count], refs[count : 2 * count]):
        lanes = slice(at, at + own.shape[2])
        k_ref[:, lanes] = (own[0].astype(F32) + other[0].astype(F32)).astype(BF16)
        v_ref[:, lanes] = (own[1].astype(F32) + other[1].astype(F32)).astype(BF16)
        at += own.shape[2]


def join(owns, others):
    shape = jax.ShapeDtypeStruct((TOK, KV_HEADS * DEPTH), BF16)
    return pl.pallas_call(
        functools.partial(join_kernel, len(owns)),
        out_shape=(shape, shape),
        compiler_params=params(),
        cost_estimate=cost(1e6, 2e6),
        name="join",
    )(*owns, *others)


def shards(
    queries, keys, values, out_grad, ssm_in, ssm_b, ssm_c, step_size, y_grad, a_log, segments, plan
):
    dp_count = lax.axis_size("dp")
    dp_index = lax.axis_index("dp")
    ctx_index = lax.axis_index("ctx")

    position = jnp.asarray(PLACE_OF, jnp.int32)
    token = jnp.arange(TOK, dtype=jnp.int32)
    own_plan = lax.dynamic_slice_in_dim(plan, dp_index, 1, 0)[0]
    goes = jnp.repeat(jnp.sum(jnp.where(own_plan[:, None] == jnp.asarray(ORDER, jnp.int32)[None, :], jnp.arange(dp_count, dtype=jnp.int32)[None, :], 0), axis=1), BLK)
    goes = goes * BLK + token % BLK
    row = jnp.stack([token, jnp.bitwise_xor(token, BLK)])
    select = (row[:, :, None] == goes[None, None, :]).astype(BF16)
    mine = jnp.sum(jnp.where(jnp.arange(dp_count, dtype=jnp.int32) == dp_index, position, 0))
    comes = jnp.sum(jnp.where(plan == dp_index, position[:, None], 0), axis=0)
    column = jnp.arange(HALVES * TOK, dtype=jnp.int32)
    half = jnp.bitwise_xor(column // TOK, mine % 2)
    arrival = jnp.tile(jnp.repeat(comes, BLK), HALVES) * PIECE + half * BLK + column % BLK
    place = (arrival[:, None] == jnp.arange(dp_count * PIECE, dtype=jnp.int32)[None, :]).astype(BF16)

    q, k, v, o = queries[0], keys[0], values[0], out_grad[0]
    x, b, c, dt, dy = ssm_in[0], ssm_b[0], ssm_c[0], step_size[0], y_grad[0]

    packed_one = pack(
        select,
        [x, dy, k, v, b, c, dt],
        [
            (0, 0, XW, True),
            (1, 0, XW, True),
            (2, 0, 256, True),
            (3, 0, 256, True),
            (4, 0, 256, True),
            (5, 0, 256, True),
            (6, 0, 128, False),
        ],
    )
    seg_row = segments[0]
    first_core = ctx_index == 0
    flag = jnp.where(first_core, 1.0, 0.0).astype(F32).reshape(1)
    seg_own = lax.dynamic_slice_in_dim(seg_row, ctx_index * TOK, TOK)
    seg_cat = jnp.concatenate([jnp.where(first_core, -1, seg_row[:TOK]), seg_own])
    biases = []
    for start in range(0, TOK, QROWS):
        key_at = start + jnp.arange(WINDOW, dtype=jnp.int32)
        query_at = TOK + start + jnp.arange(128, dtype=jnp.int32) % QROWS
        query_seg = jnp.tile(seg_cat[TOK + start : TOK + start + QROWS], 128 // QROWS)
        allowed = (key_at[:, None] <= query_at[None, :]) & (
            seg_cat[start : start + WINDOW, None] == query_seg[None, :]
        )
        biases.append(jnp.where(allowed, 0.0, MASKED).astype(F32))
    bias = jnp.stack(biases)
    at = jnp.arange(TOK, dtype=jnp.int32)
    equal = seg_own[:, None] == seg_own[None, :]
    mask = jnp.where(equal & (at[:, None] >= at[None, :]), 1.0, 0.0).astype(F32)
    turned = jnp.where(equal & (at[:, None] <= at[None, :]), 1.0, 0.0).astype(F32)
    edge = seg_row[TOK - 1]
    same = jnp.broadcast_to(jnp.where(seg_own == edge, 1.0, 0.0).astype(F32)[:, None], (TOK, MN))

    lane_head = jnp.arange(MH * MP, dtype=jnp.int32) // MP
    head = jnp.arange(2 * MH, dtype=jnp.int32) % MH
    spread = (head[:, None] == lane_head[None, :]).astype(BF16)
    gather = (lane_head[:, None] == head[None, :MH]).astype(BF16)

    received_one = exchange(packed_one)
    packed_two = pack(select, [x, dy], [(0, 2 * XW, XW, True), (1, 2 * XW, XW, True)])
    packed_three = pack(
        select,
        [q, o],
        [(0, 0, QW, True), (1, 0, QW, True), (0, 2 * QW, QW // 2, True), (1, 2 * QW, QW // 2, True)],
    )
    packed_four = pack(
        select, [q, o], [(0, 3 * QW, QW // 2, True), (1, 3 * QW, QW // 2, True)], spare=MH
    )
    made = (place, bias, mask, turned, same, spread, gather)
    packed_two, packed_three, packed_four, received_one, made = lax.optimization_barrier(
        (packed_two, packed_three, packed_four, received_one, made)
    )
    place, bias, mask, turned, same, spread, gather = made
    received_two = exchange(packed_two)

    a_row = a_log.reshape(1, MH)
    kv_own, bc, steps, e_two, f_two, columns = small(received_one, place, a_row, same, flag)
    kv_before = lax.ppermute(kv_own, "ctx", [(0, 1)])

    def states_of(received, first_group):
        x_low, dy_low, sent = state(received, first_group, 2, place, e_two, f_two, columns, spread, flag)
        return x_low, dy_low, lax.ppermute(sent, "ctx", [(0, 1), (1, 0)])

    def scanned(rows_and_states, first_group, before):
        x_low, dy_low, states = rows_and_states
        return scan(
            x_low, dy_low, first_group, 2, bc, columns, states, e_two, f_two,
            mask, turned, same, spread, gather, flag, before,
        )

    *grads_one, sums_one = scanned(states_of(received_one, 0), 0, None)
    packed_three, received_two, sums_one = lax.optimization_barrier(
        (packed_three, received_two, sums_one)
    )
    received_three = exchange(packed_three)
    dx, db, dc, sums_two = scanned(states_of(received_two, 2), 2, grads_one)
    step_grad, decay = finish(sums_one, sums_two, steps, a_row)
    packed_four, received_three = lax.optimization_barrier(
        (fill_slot(decay, packed_four), received_three)
    )
    received_four = exchange(packed_four)

    dq, own_one, before_one = attention(
        received_three, 0, 0, 2, place, kv_own, kv_before, bias, None
    )
    other_one = lax.ppermute(before_one, "ctx", [(1, 0)])
    dq, own_two, before_two = attention(
        received_three, 4, 2, 1, place, kv_own, kv_before, bias, dq
    )
    other_two = lax.ppermute(before_two, "ctx", [(1, 0)])
    dq, own_three, before_three = attention(
        received_four, 0, 3, 1, place, kv_own, kv_before, bias, dq
    )
    before_three, received_four = lax.optimization_barrier((before_three, received_four))
    other_three = lax.ppermute(before_three, "ctx", [(1, 0)])
    decay_here = sum_slots(received_four)
    decay_there = lax.ppermute(decay_here, "ctx", [(0, 1), (1, 0)])
    a_log_grad = (decay_here + decay_there).reshape(MH)
    k_grad, v_grad = join([own_one, own_two, own_three], [other_one, other_two, other_three])
    return (
        dq[None],
        k_grad[None],
        v_grad[None],
        dx[None],
        db[None],
        dc[None],
        step_grad[None],
        a_log_grad,
    )


def solution(mesh):
    tokens = P("dp", "ctx", None)
    return jax.shard_map(
        shards,
        mesh=mesh,
        in_specs=(tokens,) * 9 + (P(), P("dp", None), P()),
        out_specs=(tokens,) * 7 + (P(),),
        check_vma=False,
    )
```

profile of v0, /device:TPU:1, one launch (start us, length us, event | category | flops | bytes accessed | tf_op | source)
XLA Modules:
  0.0 231.6 jit_solution(869990704210661075)
XLA Ops:
  3.3 6.0 %pack.7 = bf16[32,16,5248]{2,1,0:T(8,128)(2,1)} custom-call(bf16[2,256,256]{2,1,0:T(8,128)(2,1)} %compare_convert_fusion.2.refs_0_, bf16[256,8192]{1,0:T(8,128)(2,1)} %bitcast.54, bf16[256,8192]{1,0:T(8,128)(2,1)} %bitcast.56, bf16[256,512]{1,0:T(8,128)(2,1)} %bitcast.70, bf16[256,512]{1,0:T(8,128)(2,1)} %bitcast.71, bf16[256,512]{1,0:T(8,128)(2,1)} %bitcast.72, ...), custom_call_target="tpu_custom_call" | custom-call | flops 1375731712 | bytes 10747904 | tf_op jit(solution)/shard_map/pack/pallas_call | solution.py:115
  9.3 12.2 %all-to-all-start = ((bf16[64,8,5248]{2,1,0:T(8,128)(2,1)}), bf16[64,8,5248]{2,1,0:T(8,128)(2,1)}, u32[]{:S(2)}, u32[]{:S(2)}) async-start(bf16[64,8,5248]{2,1,0:T(8,128)(2,1)} %bitcast.52), calls=%async_computation | async-start | bytes 10747904 | tf_op jit(solution)/shard_map/all_to_all | solution.py:136
  24.4 5.1 %pack.4 = bf16[32,16,4096]{2,1,0:T(8,128)(2,1)} custom-call(bf16[2,256,256]{2,1,0:T(8,128)(2,1)} %compare_convert_fusion.2.refs_0_, bf16[256,8192]{1,0:T(8,128)(2,1)} %bitcast.55, bf16[256,8192]{1,0:T(8,128)(2,1)} %bitcast.57), custom_call_target="tpu_custom_call" | custom-call | flops 1073741824 | bytes 8388608 | tf_op jit(solution)/shard_map/pack/pallas_call | solution.py:115
  32.1 4.6 %pack.5 = bf16[32,16,3072]{2,1,0:T(8,128)(2,1)} custom-call(bf16[2,256,256]{2,1,0:T(8,128)(2,1)} %compare_convert_fusion.2.refs_0_, bf16[256,4096]{1,0:T(8,128)(2,1)} %bitcast.59, bf16[256,4096]{1,0:T(8,128)(2,1)} %bitcast.61), custom_call_target="tpu_custom_call" | custom-call | flops 805306368 | bytes 6291456 | tf_op jit(solution)/shard_map/pack/pallas_call | solution.py:115
  37.1 3.5 %pack.6._ = bf16[32,16,1152]{2,1,0:T(8,128)(2,1)} custom-call(bf16[2,256,256]{2,1,0:T(8,128)(2,1)} %compare_convert_fusion.2.refs_0_, bf16[256,4096]{1,0:T(8,128)(2,1)} %bitcast.60, bf16[256,4096]{1,0:T(8,128)(2,1)} %bitcast.62), custom_call_target="tpu_custom_call" | custom-call | flops 301989888 | bytes 2359296 | tf_op jit(solution)/shard_map/pack/pallas_call | solution.py:115
  43.2 4.6 %compare_convert_fusion.1.refs_12_ = bf16[8192,128]{1,0:T(8,128)(2,1)} fusion(s32[128]{0:T(128)S(1)} %slice-done, s32[8192]{0:T(1024)S(1)} %add_select_fusion), kind=kLoop, calls=%fused_computation.1 | loop fusion | flops 2097152 | bytes 2130432 | tf_op jit(solution)/shard_map/convert_element_type | solution.py:612
  47.9 2.9 %compare_convert_fusion.spread.refs_11_ = bf16[256,8192]{1,0:T(8,128)(2,1)} fusion(s32[8192]{0:T(1024)S(1)} %add_select_fusion, s32[256]{0:T(256)S(1)} %copy-done.9), kind=kLoop, calls=%fused_computation | loop fusion | flops 4194304 | bytes 4228096 | tf_op jit(solution)/shard_map/convert_element_type | solution.py:611
  50.7 34.6 %all-to-all-done = bf16[64,8,5248]{2,1,0:T(8,128)(2,1)} async-done(((bf16[64,8,5248]{2,1,0:T(8,128)(2,1)}), bf16[64,8,5248]{2,1,0:T(8,128)(2,1)}, u32[]{:S(2)}, u32[]{:S(2)}) %all-to-all-start) | async-done | bytes 5373984 | tf_op jit(solution)/shard_map/all_to_all | solution.py:136
  86.1 7.1 %all-to-all-start.1 = ((bf16[64,8,4096]{2,1,0:T(8,128)(2,1)}), bf16[64,8,4096]{2,1,0:T(8,128)(2,1)}, u32[]{:S(2)}, u32[]{:S(2)}) async-start(bf16[64,8,4096]{2,1,0:T(8,128)(2,1)} %bitcast.53), calls=%async_computation.1 | async-start | bytes 8388608 | tf_op jit(solution)/shard_map/all_to_all | solution.py:136
  93.2 3.3 %small.1 = (bf16[256,1024]{1,0:T(8,128)(2,1)}, bf16[256,1024]{1,0:T(8,128)(2,1)}, f32[256,128]{1,0:T(8,128)}, bf16[256,256]{1,0:T(8,128)(2,1)}, bf16[256,256]{1,0:T(8,128)(2,1)}, /*index=5*/bf16[256,512]{1,0:T(8,128)(2,1)}) custom-call(bf16[512,5248]{1,0:T(8,128)(2,1)} %bitcast.11.r_ref.step_ref.xr_ref.dyr_ref, ...), custom_call_target="tpu_custom_call" | custom-call | flops 603979776 | bytes 4000000 | tf_op jit(solution)/shard_map/small/pallas_call | solution.py:170
  96.5 9.0 %state.2 = (bf16[256,4096]{1,0:T(8,128)(2,1)}, bf16[256,4096]{1,0:T(8,128)(2,1)}, bf16[128,4096]{1,0:T(8,128)(2,1)}) custom-call(bf16[512,5248]{1,0:T(8,128)(2,1)} %bitcast.11.r_ref.step_ref.xr_ref.dyr_ref, bf16[512,5248]{1,0:T(8,128)(2,1)} %bitcast.11.r_ref.step_ref.xr_ref.dyr_ref, bf16[512,512]{1,0:T(8,128)(2,1)} %fusion.place_ref.refs_2_, ...), custom_call_target="tpu_custom_call" | custom-call | flops 6000000000 | bytes 14000000 | tf_op jit(solution)/shard_map/state/pallas_call | solution.py:316
  105.5 2.1 collective-permute-start
  107.5 2.5 %collective-permute-done.refs_5_ = bf16[128,4096]{1,0:T(8,128)(2,1)S(1)} collective-permute-done((bf16[128,4096]{1,0:T(8,128)(2,1)}, bf16[128,4096]{1,0:T(8,128)(2,1)S(1)}, u32[]{:S(2)}, u32[]{:S(2)}) %collective-permute-start) | collective-permute-done | bytes 1048608 | tf_op jit(solution)/shard_map/ppermute | solution.py:637
  111.0 13.2 %scan.2 = (bf16[256,8192]{1,0:T(8,128)(2,1)}, bf16[256,512]{1,0:T(8,128)(2,1)}, bf16[256,512]{1,0:T(8,128)(2,1)}, f32[2,256,128]{2,1,0:T(8,128)}) custom-call(bf16[256,4096]{1,0:T(8,128)(2,1)} %get-tuple-element.68.refs_0_, bf16[256,4096]{1,0:T(8,128)(2,1)} %get-tuple-element.69.refs_1_, bf16[256,1024]{1,0:T(8,128)(2,1)} %get-tuple-element.70.refs_2_.refs_3_, ...), custom_call_target="tpu_custom_call" | custom-call | flops 8000000000 | bytes 10000000 | tf_op jit(solution)/shard_map/scan/pallas_call | solution.py:431
  124.2 18.9 %all-to-all-done.1 = bf16[64,8,4096]{2,1,0:T(8,128)(2,1)} async-done(((bf16[64,8,4096]{2,1,0:T(8,128)(2,1)}), bf16[64,8,4096]{2,1,0:T(8,128)(2,1)}, u32[]{:S(2)}, u32[]{:S(2)}) %all-to-all-start.1) | async-done | bytes 4194336 | tf_op jit(solution)/shard_map/all_to_all | solution.py:136
  143.1 6.2 %all-to-all-start.2 = ((bf16[64,8,3072]{2,1,0:T(8,128)(2,1)}), bf16[64,8,3072]{2,1,0:T(8,128)(2,1)S(1)}, u32[]{:S(2)}, u32[]{:S(2)}) async-start(bf16[64,8,3072]{2,1,0:T(8,128)(2,1)} %bitcast.27), calls=%async_computation.2 | async-start | bytes 6291456 | tf_op jit(solution)/shard_map/all_to_all | solution.py:136
  149.4 9.0 %state.3 = (bf16[256,4096]{1,0:T(8,128)(2,1)}, bf16[256,4096]{1,0:T(8,128)(2,1)}, bf16[128,4096]{1,0:T(8,128)(2,1)}) custom-call(bf16[512,4096]{1,0:T(8,128)(2,1)} %bitcast.24.xr_ref.dyr_ref, bf16[512,4096]{1,0:T(8,128)(2,1)} %bitcast.24.xr_ref.dyr_ref, bf16[512,512]{1,0:T(8,128)(2,1)} %fusion.place_ref.refs_2_, ...), custom_call_target="tpu_custom_call" | custom-call | flops 6000000000 | bytes 14000000 | tf_op jit(solution)/shard_map/state/pallas_call | solution.py:316
  158.4 1.8 collective-permute-start.1
  160.2 1.5 collective-permute-start.2
  163.7 13.2 %scan.3 = (bf16[256,8192]{1,0:T(8,128)(2,1)}, bf16[256,512]{1,0:T(8,128)(2,1)}, bf16[256,512]{1,0:T(8,128)(2,1)}, f32[2,256,128]{2,1,0:T(8,128)}) custom-call(bf16[256,4096]{1,0:T(8,128)(2,1)} %get-tuple-element.78.refs_0_, bf16[256,4096]{1,0:T(8,128)(2,1)} %get-tuple-element.79.refs_1_, ...), custom_call_target="tpu_custom_call", output_to_operand_aliasing={{0}: (14, {}), {1}: (15, {}), {2}: (16, {})} | custom-call | flops 8000000000 | bytes 10000000 | tf_op jit(solution)/shard_map/scan/pallas_call | solution.py:431
  176.9 2.0 finish.1
  180.2 8.5 %all-to-all-done.2 = bf16[64,8,3072]{2,1,0:T(8,128)(2,1)S(1)} async-done(((bf16[64,8,3072]{2,1,0:T(8,128)(2,1)}), bf16[64,8,3072]{2,1,0:T(8,128)(2,1)S(1)}, u32[]{:S(2)}, u32[]{:S(2)}) %all-to-all-start.2) | async-done | bytes 3145760 | tf_op jit(solution)/shard_map/all_to_all | solution.py:136
  188.7 1.7 copy-done.1
  190.4 5.2 %all-to-all-start.3 = ((bf16[64,8,1152]{2,1,0:T(8,128)(2,1)}), bf16[64,8,1152]{2,1,0:T(8,128)(2,1)S(1)}, u32[]{:S(2)}, u32[]{:S(2)}) async-start(bf16[64,8,1152]{2,1,0:T(8,128)(2,1)} %bitcast.58), calls=%async_computation.3 | async-start | bytes 2359296 | tf_op jit(solution)/shard_map/all_to_all | solution.py:136
  195.6 8.3 %attention.3 = (bf16[256,4096]{1,0:T(8,128)(2,1)}, bf16[2,256,256]{2,1,0:T(8,128)(2,1)}, bf16[2,256,256]{2,1,0:T(8,128)(2,1)}) custom-call(bf16[512,3072]{1,0:T(8,128)(2,1)} %bitcast.66, bf16[512,3072]{1,0:T(8,128)(2,1)} %bitcast.67, bf16[512,512]{1,0:T(8,128)(2,1)} %fusion.place_ref.refs_2_, bf16[256,1024]{1,0:T(8,128)(2,1)} %get-tuple-element.90.refs_3_.refs_4_, ...), custom_call_target="tpu_custom_call" | custom-call | flops 12000000000 | bytes 8000000 | tf_op jit(solution)/shard_map/attention/pallas_call | solution.py:270
  204.0 4.8 %collective-permute-start.3 = (bf16[2,256,256]{2,1,0:T(8,128)(2,1)}, bf16[2,256,256]{2,1,0:T(8,128)(2,1)S(1)}, u32[]{:S(2)}, u32[]{:S(2)}) collective-permute-start(bf16[2,256,256]{2,1,0:T(8,128)(2,1)} %get-tuple-element.99), channel_id=1, source_target_pairs={{1,0},{3,2},{5,4},{7,6},{9,8},{11,10},{13,12},{15,14},{17,16},{19,... | collective-permute-start | bytes 786440 | tf_op jit(solution)/shard_map/ppermute | solution.py:661
  208.8 5.3 %attention.4 = (bf16[256,4096]{1,0:T(8,128)(2,1)}, bf16[2,256,128]{2,1,0:T(8,128)(2,1)}, bf16[2,256,128]{2,1,0:T(8,128)(2,1)}) custom-call(bf16[512,3072]{1,0:T(8,128)(2,1)} %bitcast.68, bf16[512,3072]{1,0:T(8,128)(2,1)} %bitcast.69, bf16[512,512]{1,0:T(8,128)(2,1)} %fusion.place_ref.refs_2_, ...), custom_call_target="tpu_custom_call", output_to_operand_aliasing={{0}: (8, {})} | custom-call | flops 6000000000 | bytes 4000000 | tf_op jit(solution)/shard_map/attention/pallas_call | solution.py:270
  215.1 5.3 %attention.5 = (bf16[256,4096]{1,0:T(8,128)(2,1)}, bf16[2,256,128]{2,1,0:T(8,128)(2,1)}, bf16[2,256,128]{2,1,0:T(8,128)(2,1)}) custom-call(bf16[512,1152]{1,0:T(8,128)(2,1)} %bitcast.63, bf16[512,1152]{1,0:T(8,128)(2,1)} %bitcast.64, bf16[512,512]{1,0:T(8,128)(2,1)} %fusion.place_ref.refs_2_, ...), custom_call_target="tpu_custom_call", output_to_operand_aliasing={{0}: (8, {})} | custom-call | flops 6000000000 | bytes 4000000 | tf_op jit(solution)/shard_map/attention/pallas_call | solution.py:270
  220.4 1.5 sum_slots.1
  221.9 2.4 %collective-permute-start.6 = (f32[1,128]{1,0:T(1,128)}, f32[1,128]{1,0:T(1,128)S(1)}, u32[]{:S(2)}, u32[]{:S(2)}) collective-permute-start(f32[1,128]{1,0:T(1,128)} %sum_slots.1), channel_id=1, source_target_pairs={{0,1},{1,0},{2,3},{3,2},{4,5},{5,4},{6,7},{7,6},{8,9},{9,8},{10,11... | collective-permute-start | bytes 1544 | tf_op jit(solution)/shard_map/ppermute | solution.py:672
  224.3 1.9 collective-permute-start.4
  229.5 2.1 join.1
  (103 shorter events, 18.1 us)
Async XLA Ops:
  9.3 12.4 %copy-start.10 = (s32[64]{0:T(128)S(1)}, s32[64]{0:T(128)}, u32[]{:S(2)}) copy-start(s32[64]{0:T(128)} %constant.175.clone) | copy-start | bytes 772
  9.3 14.9 %copy-start.5 = (s32[64,64]{1,0:T(8,128)S(1)}, s32[64,64]{1,0:T(8,128)}, u32[]{:S(2)}) copy-start(s32[64,64]{1,0:T(8,128)} %param.25) | copy-start | bytes 49156
  9.3 76.0 %all-to-all-start = ((bf16[64,8,5248]{2,1,0:T(8,128)(2,1)}), bf16[64,8,5248]{2,1,0:T(8,128)(2,1)}, u32[]{:S(2)}, u32[]{:S(2)}) async-start(bf16[64,8,5248]{2,1,0:T(8,128)(2,1)} %bitcast.52), calls=%async_computation | async-start | bytes 10747904 | tf_op jit(solution)/shard_map/all_to_all | solution.py:136
  24.3 5.1 %copy-start.6 = (s32[1,512]{1,0:T(1,128)S(1)}, s32[1,512]{1,0:T(1,128)}, u32[]{:S(2)}) copy-start(s32[1,512]{1,0:T(1,128)} %param.24) | copy-start | bytes 6148
  29.5 7.6 %copy-start.8 = (s32[256]{0:T(256)}, s32[256]{0:T(256)S(1)}, u32[]{:S(2)}) copy-start(s32[256]{0:T(256)S(1)} %and_select_fusion) | copy-start | bytes 3076
  37.0 6.2 %slice-start = ((s32[256]{0:T(256)}), s32[128]{0:T(128)S(1)}, s32[]{:S(2)}) async-start(s32[256]{0:T(256)} %copy-done.8), calls=%async_computation.4 | async-start | bytes 1024 | tf_op jit(solution)/shard_map/slice | solution.py:612
  40.5 7.3 %copy-start.9 = (s32[256]{0:T(256)S(1)}, s32[256]{0:T(256)}, u32[]{:S(2)}) copy-start(s32[256]{0:T(256)} %copy-done.8) | copy-start | bytes 3076
  41.2 9.6 %copy-start.7 = (f32[8,288,128]{2,1,0:T(8,128)}, f32[8,288,128]{2,1,0:T(8,128)S(1)}, u32[]{:S(2)}) copy-start(f32[8,288,128]{2,1,0:T(8,128)S(1)} %select_dynamic-update-slice_fusion.refs_7_) | copy-start | bytes 3538948
  86.1 57.1 %all-to-all-start.1 = ((bf16[64,8,4096]{2,1,0:T(8,128)(2,1)}), bf16[64,8,4096]{2,1,0:T(8,128)(2,1)}, u32[]{:S(2)}, u32[]{:S(2)}) async-start(bf16[64,8,4096]{2,1,0:T(8,128)(2,1)} %bitcast.53), calls=%async_computation.1 | async-start | bytes 8388608 | tf_op jit(solution)/shard_map/all_to_all | solution.py:136
  105.5 4.6 %collective-permute-start = (bf16[128,4096]{1,0:T(8,128)(2,1)}, bf16[128,4096]{1,0:T(8,128)(2,1)S(1)}, u32[]{:S(2)}, u32[]{:S(2)}) collective-permute-start(bf16[128,4096]{1,0:T(8,128)(2,1)} %get-tuple-element.71), channel_id=1, source_target_pairs={{0,1},{1,0},{2,3},{3,2},{4,5},{5,4},{6,7},{7,6},{8,9},{9,8},{10,11... | collective-permute-start | bytes 3145736 | tf_op jit(solution)/shard_map/ppermute | solution.py:637
  110.0 1.0 copy-start.12
  143.1 45.6 %all-to-all-start.2 = ((bf16[64,8,3072]{2,1,0:T(8,128)(2,1)}), bf16[64,8,3072]{2,1,0:T(8,128)(2,1)S(1)}, u32[]{:S(2)}, u32[]{:S(2)}) async-start(bf16[64,8,3072]{2,1,0:T(8,128)(2,1)} %bitcast.27), calls=%async_computation.2 | async-start | bytes 6291456 | tf_op jit(solution)/shard_map/all_to_all | solution.py:136
  158.4 4.3 %collective-permute-start.1 = (bf16[128,4096]{1,0:T(8,128)(2,1)}, bf16[128,4096]{1,0:T(8,128)(2,1)S(1)}, u32[]{:S(2)}, u32[]{:S(2)}) collective-permute-start(bf16[128,4096]{1,0:T(8,128)(2,1)} %get-tuple-element.80), channel_id=1, source_target_pairs={{0,1},{1,0},{2,3},{3,2},{4,5},{5,4},{6,7},{7,6},{8,9},{9,8},{10,11... | collective-permute-start | bytes 3145736 | tf_op jit(solution)/shard_map/ppermute | solution.py:637
  160.2 35.4 %collective-permute-start.2 = (bf16[256,1024]{1,0:T(8,128)(2,1)}, bf16[256,1024]{1,0:T(8,128)(2,1)}, u32[]{:S(2)}, u32[]{:S(2)}) collective-permute-start(bf16[256,1024]{1,0:T(8,128)(2,1)} %get-tuple-element.90.refs_3_.refs_4_), channel_id=1, source_target_pairs={{0,1},{2,3},{4,5},{6,7},{8,9},{10,11},{12,13},{14,15},{16,17},{18,... | collective-permute-start | bytes 1572872 | tf_op jit(solution)/shard_map/ppermute | solution.py:633
  162.7 1.0 copy-start.11
  188.7 1.8 copy-start.1
  190.4 23.7 %all-to-all-start.3 = ((bf16[64,8,1152]{2,1,0:T(8,128)(2,1)}), bf16[64,8,1152]{2,1,0:T(8,128)(2,1)S(1)}, u32[]{:S(2)}, u32[]{:S(2)}) async-start(bf16[64,8,1152]{2,1,0:T(8,128)(2,1)} %bitcast.58), calls=%async_computation.3 | async-start | bytes 2359296 | tf_op jit(solution)/shard_map/all_to_all | solution.py:136
  204.0 24.7 %collective-permute-start.3 = (bf16[2,256,256]{2,1,0:T(8,128)(2,1)}, bf16[2,256,256]{2,1,0:T(8,128)(2,1)S(1)}, u32[]{:S(2)}, u32[]{:S(2)}) collective-permute-start(bf16[2,256,256]{2,1,0:T(8,128)(2,1)} %get-tuple-element.99), channel_id=1, source_target_pairs={{1,0},{3,2},{5,4},{7,6},{9,8},{11,10},{13,12},{15,14},{17,16},{19,... | collective-permute-start | bytes 786440 | tf_op jit(solution)/shard_map/ppermute | solution.py:661
  214.1 1.0 copy-start
  215.1 9.2 %copy-start.13 = (bf16[2,256,128]{2,1,0:T(8,128)(2,1)S(1)}, bf16[2,256,128]{2,1,0:T(8,128)(2,1)}, u32[]{:S(2)}) copy-start(bf16[2,256,128]{2,1,0:T(8,128)(2,1)} %get-tuple-element.100) | copy-start | bytes 393220
  221.9 5.6 %collective-permute-start.6 = (f32[1,128]{1,0:T(1,128)}, f32[1,128]{1,0:T(1,128)S(1)}, u32[]{:S(2)}, u32[]{:S(2)}) collective-permute-start(f32[1,128]{1,0:T(1,128)} %sum_slots.1), channel_id=1, source_target_pairs={{0,1},{1,0},{2,3},{3,2},{4,5},{5,4},{6,7},{7,6},{8,9},{9,8},{10,11... | collective-permute-start | bytes 1544 | tf_op jit(solution)/shard_map/ppermute | solution.py:672
  224.3 4.3 %collective-permute-start.4 = (bf16[2,256,128]{2,1,0:T(8,128)(2,1)S(1)}, bf16[2,256,128]{2,1,0:T(8,128)(2,1)S(1)}, u32[]{:S(2)}, u32[]{:S(2)}) collective-permute-start(bf16[2,256,128]{2,1,0:T(8,128)(2,1)S(1)} %copy-done.13), channel_id=1, source_target_pairs={{1,0},{3,2},{5,4},{7,6},{9,8},{11,10},{13,12},{15,14},{17,16},{19,... | collective-permute-start | bytes 393224 | tf_op jit(solution)/shard_map/ppermute | solution.py:665
  226.2 2.5 %collective-permute-start.5 = (bf16[2,256,128]{2,1,0:T(8,128)(2,1)}, bf16[2,256,128]{2,1,0:T(8,128)(2,1)S(1)}, u32[]{:S(2)}, u32[]{:S(2)}) collective-permute-start(bf16[2,256,128]{2,1,0:T(8,128)(2,1)} %get-tuple-element.102), channel_id=1, source_target_pairs={{1,0},{3,2},{5,4},{7,6},{9,8},{11,10},{13,12},{15,14},{17,16},{19,... | collective-permute-start | bytes 393224 | tf_op jit(solution)/shard_map/ppermute | solution.py:670
  228.7 0.6 copy-start.3
  228.7 0.7 copy-start.2
  228.7 0.8 copy-start.4
where the time goes:
time: 233 us; the launch traced here: 232 us
  Pallas kernels  92.6 us (40%)
  waiting for transfers between devices  65.5 us (28%)
  starting transfers between devices  46.6 us (20%)
  other arithmetic  15 us (6%)
  local copies, waits for them, and re-layouts  8.76 us (4%)
  between operations  3.09 us (1%)
    all_to_all x4, waiting for transfers between devices, exchange(): lax.all_to_all(pieces, 'dp', split_axis=0, concat_axis=0, tiled=True, axi...  62 us
    all_to_all x4, starting transfers between devices, exchange(): lax.all_to_all(pieces, 'dp', split_axis=0, concat_axis=0, tiled=True, axi...  30.8 us
    pallas_call x2, Pallas kernels, scan(): pl.pallas_call(scan_kernel, grid=(groups,), out_shape=(jax.ShapeDtypeStru...  26.3 us
    pallas_call x4, Pallas kernels, pack(): pl.pallas_call(functools.partial(pack_kernel, jobs, len(arrays)), out_sha...  19.2 us
    pallas_call x3, Pallas kernels, attention(): pl.pallas_call(functools.partial(attention_kernel, split), grid=(groups,)...  18.9 us
    pallas_call x2, Pallas kernels, state(): pl.pallas_call(state_kernel, grid=(groups,), out_shape=(jax.ShapeDtypeStr...  18 us
    unnamed x30, local copies, waits for them, and re-layouts  5.56 us
    ppermute x1, starting transfers between devices, shards(): other_one = lax.ppermute(before_one, 'ctx', [(1, 0)])  4.84 us
  transfers between devices with their start and end apart: 11, of which 5 were waited for; matrix products, arithmetic and copies ran while one was open for 6% of the time, Pallas kernels for 36%

commit v1 on v0

--- a/solution.py
+++ b/solution.py
@@ -246,7 +246,7 @@
     own_ref[1] = dv[TOK:].astype(BF16)
 
 
-def attention(received, block, first_group, groups, place, kv_own, kv_before, bias, dq_before):
+def attention(received, block, first_group, groups, place, kv_own, kv_before, bias, earlier):
     split = groups == 1
     width, rows = (QW // 2, 2 * TOK) if split else (QW, TOK)
     key_at = lambda g: (0, first_group + g)
@@ -263,23 +263,23 @@
     ]
     operands = [received, received, place, kv_own, kv_own, kv_before, kv_before, bias]
     aliases = {}
-    if dq_before is not None:
-        in_specs.append(pl.BlockSpec(memory_space=pl.ANY))
-        operands.append(dq_before)
-        aliases = {8: 0}
+    if earlier is not None:
+        in_specs += [pl.BlockSpec(memory_space=pl.ANY)] * 3
+        operands += list(earlier)
+        aliases = {8: 0, 9: 1, 10: 2}
     return pl.pallas_call(
         functools.partial(attention_kernel, split),
         grid=(groups,),
         out_shape=(
             jax.ShapeDtypeStruct((TOK, KV_HEADS * QW), BF16),
-            jax.ShapeDtypeStruct((2, TOK, groups * DEPTH), BF16),
-            jax.ShapeDtypeStruct((2, TOK, groups * DEPTH), BF16),
+            jax.ShapeDtypeStruct((2, TOK, KV_HEADS * DEPTH), BF16),
+            jax.ShapeDtypeStruct((2, TOK, KV_HEADS * DEPTH), BF16),
         ),
         in_specs=in_specs,
         out_specs=(
             pl.BlockSpec((TOK, QW), lambda g: (0, first_group + g)),
-            pl.BlockSpec((2, TOK, DEPTH), lambda g: (0, 0, g)),
-            pl.BlockSpec((2, TOK, DEPTH), lambda g: (0, 0, g)),
+            pl.BlockSpec((2, TOK, DEPTH), lambda g: (0, 0, first_group + g)),
+            pl.BlockSpec((2, TOK, DEPTH), lambda g: (0, 0, first_group + g)),
         ),
         scratch_shapes=[
             pltpu.VMEM((TOK, 2 * QW), BF16),
@@ -526,25 +526,20 @@
     )(received)
 
 
-def join_kernel(count, *refs):
-    k_ref, v_ref = refs[-2:]
-    at = 0
-    for own, other in zip(refs[:count], refs[count : 2 * count]):
-        lanes = slice(at, at + own.shape[2])
-        k_ref[:, lanes] = (own[0].astype(F32) + other[0].astype(F32)).astype(BF16)
-        v_ref[:, lanes] = (own[1].astype(F32) + other[1].astype(F32)).astype(BF16)
-        at += own.shape[2]
-
-
-def join(owns, others):
+def join_kernel(own_ref, other_ref, k_ref, v_ref):
+    k_ref[...] = (own_ref[0].astype(F32) + other_ref[0].astype(F32)).astype(BF16)
+    v_ref[...] = (own_ref[1].astype(F32) + other_ref[1].astype(F32)).astype(BF16)
+
+
+def join(own, other):
     shape = jax.ShapeDtypeStruct((TOK, KV_HEADS * DEPTH), BF16)
     return pl.pallas_call(
-        functools.partial(join_kernel, len(owns)),
+        join_kernel,
         out_shape=(shape, shape),
         compiler_params=params(),
         cost_estimate=cost(1e6, 2e6),
         name="join",
-    )(*owns, *others)
+    )(own, other)
 
 
 def shards(
@@ -655,23 +650,17 @@
     )
     received_four = exchange(packed_four)
 
-    dq, own_one, before_one = attention(
-        received_three, 0, 0, 2, place, kv_own, kv_before, bias, None
-    )
-    other_one = lax.ppermute(before_one, "ctx", [(1, 0)])
-    dq, own_two, before_two = attention(
-        received_three, 4, 2, 1, place, kv_own, kv_before, bias, dq
-    )
-    other_two = lax.ppermute(before_two, "ctx", [(1, 0)])
-    dq, own_three, before_three = attention(
-        received_four, 0, 3, 1, place, kv_own, kv_before, bias, dq
-    )
-    before_three, received_four = lax.optimization_barrier((before_three, received_four))
-    other_three = lax.ppermute(before_three, "ctx", [(1, 0)])
+    terms = attention(received_three, 0, 0, 2, place, kv_own, kv_before, bias, None)
+    terms = attention(received_three, 4, 2, 1, place, kv_own, kv_before, bias, terms)
+    dq, own, before = attention(
+        received_four, 0, 3, 1, place, kv_own, kv_before, bias, terms
+    )
+    before, received_four = lax.optimization_barrier((before, received_four))
+    other = lax.ppermute(before, "ctx", [(1, 0)])
     decay_here = sum_slots(received_four)
     decay_there = lax.ppermute(decay_here, "ctx", [(0, 1), (1, 0)])
     a_log_grad = (decay_here + decay_there).reshape(MH)
-    k_grad, v_grad = join([own_one, own_two, own_three], [other_one, other_two, other_three])
+    k_grad, v_grad = join(own, other)
     return (
         dq[None],
         k_grad[None],

time: 233 us -> 232 us (level)
  starting transfers between devices: 46.6 us -> 41.8 us
  waiting for transfers between devices: 65.5 us -> 70.1 us
    all_to_all x4, waiting for transfers between devices: 62 us -> 65.4 us  [exchange(): lax.all_to_all(pieces, 'dp', split_axis=0, concat_axis=0, tiled=True, axi...]
    ppermute x3 -> x1, starting transfers between devices: 8.04 us -> 5.59 us  [shards(): other = lax.ppermute(before, 'ctx', [(1, 0)])]
    ppermute x1, starting transfers between devices: 2.39 us -> 0.01 us  [shards(): decay_there = lax.ppermute(decay_here, 'ctx', [(0, 1), (1, 0)])]
    unnamed x30 -> x24, local copies, waits for them, and re-layouts: 5.56 us -> 5.58 us
  transfers between devices with their start and end apart: 11 -> 9, of which waited for: 5 -> 7; matrix products, arithmetic and copies ran while one was open for 6% -> 6% of each run, Pallas kernels for 36% -> 34%
where the time goes in v1:
time: 232 us; the launch traced here: 231 us
  Pallas kernels  92.7 us (40%)
  waiting for transfers between devices  70.1 us (30%)
  starting transfers between devices  41.8 us (18%)
  other arithmetic  15.1 us (7%)
  local copies, waits for them, and re-layouts  8.78 us (4%)
  between operations  3.05 us (1%)
    all_to_all x4, waiting for transfers between devices, exchange(): lax.all_to_all(pieces, 'dp', split_axis=0, concat_axis=0, tiled=True, axi...  65.4 us
    all_to_all x4, starting transfers between devices, exchange(): lax.all_to_all(pieces, 'dp', split_axis=0, concat_axis=0, tiled=True, axi...  30.8 us
    pallas_call x2, Pallas kernels, scan(): pl.pallas_call(scan_kernel, grid=(groups,), out_shape=(jax.ShapeDtypeStru...  26.4 us
    pallas_call x4, Pallas kernels, pack(): pl.pallas_call(functools.partial(pack_kernel, jobs, len(arrays)), out_sha...  19.3 us
    pallas_call x3, Pallas kernels, attention(): pl.pallas_call(functools.partial(attention_kernel, split), grid=(groups,)...  18.9 us
    pallas_call x2, Pallas kernels, state(): pl.pallas_call(state_kernel, grid=(groups,), out_shape=(jax.ShapeDtypeStr...  18 us
    ppermute x1, starting transfers between devices, shards(): other = lax.ppermute(before, 'ctx', [(1, 0)])  5.59 us
    unnamed x24, local copies, waits for them, and re-layouts  5.58 us
  transfers between devices with their start and end apart: 9, of which 7 were waited for; matrix products, arithmetic and copies ran while one was open for 6% of the time, Pallas kernels for 34%

profile of v1, /device:TPU:1, one launch (start us, length us, event | category | flops | bytes accessed | tf_op | source)
XLA Modules:
  0.0 231.5 jit_solution(15945803827439048852)
XLA Ops:
  3.3 6.1 %pack.7 = bf16[32,16,5248]{2,1,0:T(8,128)(2,1)} custom-call(bf16[2,256,256]{2,1,0:T(8,128)(2,1)} %compare_convert_fusion.2.refs_0_, bf16[256,8192]{1,0:T(8,128)(2,1)} %bitcast.54, bf16[256,8192]{1,0:T(8,128)(2,1)} %bitcast.56, bf16[256,512]{1,0:T(8,128)(2,1)} %bitcast.70, bf16[256,512]{1,0:T(8,128)(2,1)} %bitcast.71, bf16[256,512]{1,0:T(8,128)(2,1)} %bitcast.72, ...), custom_call_target="tpu_custom_call" | custom-call | flops 1375731712 | bytes 10747904 | tf_op jit(solution)/shard_map/pack/pallas_call | solution.py:115
  9.4 12.2 %all-to-all-start = ((bf16[64,8,5248]{2,1,0:T(8,128)(2,1)}), bf16[64,8,5248]{2,1,0:T(8,128)(2,1)}, u32[]{:S(2)}, u32[]{:S(2)}) async-start(bf16[64,8,5248]{2,1,0:T(8,128)(2,1)} %bitcast.52), calls=%async_computation | async-start | bytes 10747904 | tf_op jit(solution)/shard_map/all_to_all | solution.py:136
  24.4 5.1 %pack.4 = bf16[32,16,4096]{2,1,0:T(8,128)(2,1)} custom-call(bf16[2,256,256]{2,1,0:T(8,128)(2,1)} %compare_convert_fusion.2.refs_0_, bf16[256,8192]{1,0:T(8,128)(2,1)} %bitcast.55, bf16[256,8192]{1,0:T(8,128)(2,1)} %bitcast.57), custom_call_target="tpu_custom_call" | custom-call | flops 1073741824 | bytes 8388608 | tf_op jit(solution)/shard_map/pack/pallas_call | solution.py:115
  32.1 4.6 %pack.5 = bf16[32,16,3072]{2,1,0:T(8,128)(2,1)} custom-call(bf16[2,256,256]{2,1,0:T(8,128)(2,1)} %compare_convert_fusion.2.refs_0_, bf16[256,4096]{1,0:T(8,128)(2,1)} %bitcast.59, bf16[256,4096]{1,0:T(8,128)(2,1)} %bitcast.61), custom_call_target="tpu_custom_call" | custom-call | flops 805306368 | bytes 6291456 | tf_op jit(solution)/shard_map/pack/pallas_call | solution.py:115
  37.1 3.5 %pack.6._ = bf16[32,16,1152]{2,1,0:T(8,128)(2,1)} custom-call(bf16[2,256,256]{2,1,0:T(8,128)(2,1)} %compare_convert_fusion.2.refs_0_, bf16[256,4096]{1,0:T(8,128)(2,1)} %bitcast.60, bf16[256,4096]{1,0:T(8,128)(2,1)} %bitcast.62), custom_call_target="tpu_custom_call" | custom-call | flops 301989888 | bytes 2359296 | tf_op jit(solution)/shard_map/pack/pallas_call | solution.py:115
  43.4 4.6 %compare_convert_fusion.1.refs_12_ = bf16[8192,128]{1,0:T(8,128)(2,1)} fusion(s32[128]{0:T(128)S(1)} %slice-done, s32[8192]{0:T(1024)S(1)} %add_select_fusion), kind=kLoop, calls=%fused_computation.1 | loop fusion | flops 2097152 | bytes 2130432 | tf_op jit(solution)/shard_map/convert_element_type | solution.py:607
  48.0 2.9 %compare_convert_fusion.spread.refs_11_ = bf16[256,8192]{1,0:T(8,128)(2,1)} fusion(s32[8192]{0:T(1024)S(1)} %add_select_fusion, s32[256]{0:T(256)S(1)} %copy-done.7), kind=kLoop, calls=%fused_computation | loop fusion | flops 4194304 | bytes 4228096 | tf_op jit(solution)/shard_map/convert_element_type | solution.py:606
  50.9 34.4 %all-to-all-done = bf16[64,8,5248]{2,1,0:T(8,128)(2,1)} async-done(((bf16[64,8,5248]{2,1,0:T(8,128)(2,1)}), bf16[64,8,5248]{2,1,0:T(8,128)(2,1)}, u32[]{:S(2)}, u32[]{:S(2)}) %all-to-all-start) | async-done | bytes 5373984 | tf_op jit(solution)/shard_map/all_to_all | solution.py:136
  86.1 7.1 %all-to-all-start.1 = ((bf16[64,8,4096]{2,1,0:T(8,128)(2,1)}), bf16[64,8,4096]{2,1,0:T(8,128)(2,1)}, u32[]{:S(2)}, u32[]{:S(2)}) async-start(bf16[64,8,4096]{2,1,0:T(8,128)(2,1)} %bitcast.53), calls=%async_computation.1 | async-start | bytes 8388608 | tf_op jit(solution)/shard_map/all_to_all | solution.py:136
  93.2 3.3 %small.1 = (bf16[256,1024]{1,0:T(8,128)(2,1)}, bf16[256,1024]{1,0:T(8,128)(2,1)}, f32[256,128]{1,0:T(8,128)}, bf16[256,256]{1,0:T(8,128)(2,1)}, bf16[256,256]{1,0:T(8,128)(2,1)}, /*index=5*/bf16[256,512]{1,0:T(8,128)(2,1)}) custom-call(bf16[512,5248]{1,0:T(8,128)(2,1)} %bitcast.11.r_ref.step_ref.xr_ref.dyr_ref, ...), custom_call_target="tpu_custom_call" | custom-call | flops 603979776 | bytes 4000000 | tf_op jit(solution)/shard_map/small/pallas_call | solution.py:170
  96.5 9.0 %state.2 = (bf16[256,4096]{1,0:T(8,128)(2,1)}, bf16[256,4096]{1,0:T(8,128)(2,1)}, bf16[128,4096]{1,0:T(8,128)(2,1)}) custom-call(bf16[512,5248]{1,0:T(8,128)(2,1)} %bitcast.11.r_ref.step_ref.xr_ref.dyr_ref, bf16[512,5248]{1,0:T(8,128)(2,1)} %bitcast.11.r_ref.step_ref.xr_ref.dyr_ref, bf16[512,512]{1,0:T(8,128)(2,1)} %fusion.place_ref.refs_2_, ...), custom_call_target="tpu_custom_call" | custom-call | flops 6000000000 | bytes 14000000 | tf_op jit(solution)/shard_map/state/pallas_call | solution.py:316
  105.5 2.1 collective-permute-start
  107.6 2.5 %collective-permute-done.refs_5_ = bf16[128,4096]{1,0:T(8,128)(2,1)S(1)} collective-permute-done((bf16[128,4096]{1,0:T(8,128)(2,1)}, bf16[128,4096]{1,0:T(8,128)(2,1)S(1)}, u32[]{:S(2)}, u32[]{:S(2)}) %collective-permute-start) | collective-permute-done | bytes 1048608 | tf_op jit(solution)/shard_map/ppermute | solution.py:632
  111.1 13.2 %scan.2 = (bf16[256,8192]{1,0:T(8,128)(2,1)}, bf16[256,512]{1,0:T(8,128)(2,1)}, bf16[256,512]{1,0:T(8,128)(2,1)}, f32[2,256,128]{2,1,0:T(8,128)}) custom-call(bf16[256,4096]{1,0:T(8,128)(2,1)} %get-tuple-element.68.refs_0_, bf16[256,4096]{1,0:T(8,128)(2,1)} %get-tuple-element.69.refs_1_, bf16[256,1024]{1,0:T(8,128)(2,1)} %get-tuple-element.70.refs_2_.refs_3_, ...), custom_call_target="tpu_custom_call" | custom-call | flops 8000000000 | bytes 10000000 | tf_op jit(solution)/shard_map/scan/pallas_call | solution.py:431
  124.3 18.9 %all-to-all-done.1 = bf16[64,8,4096]{2,1,0:T(8,128)(2,1)} async-done(((bf16[64,8,4096]{2,1,0:T(8,128)(2,1)}), bf16[64,8,4096]{2,1,0:T(8,128)(2,1)}, u32[]{:S(2)}, u32[]{:S(2)}) %all-to-all-start.1) | async-done | bytes 4194336 | tf_op jit(solution)/shard_map/all_to_all | solution.py:136
  143.2 6.2 %all-to-all-start.2 = ((bf16[64,8,3072]{2,1,0:T(8,128)(2,1)}), bf16[64,8,3072]{2,1,0:T(8,128)(2,1)S(1)}, u32[]{:S(2)}, u32[]{:S(2)}) async-start(bf16[64,8,3072]{2,1,0:T(8,128)(2,1)} %bitcast.27), calls=%async_computation.2 | async-start | bytes 6291456 | tf_op jit(solution)/shard_map/all_to_all | solution.py:136
  149.4 9.0 %state.3 = (bf16[256,4096]{1,0:T(8,128)(2,1)}, bf16[256,4096]{1,0:T(8,128)(2,1)}, bf16[128,4096]{1,0:T(8,128)(2,1)}) custom-call(bf16[512,4096]{1,0:T(8,128)(2,1)} %bitcast.24.xr_ref.dyr_ref, bf16[512,4096]{1,0:T(8,128)(2,1)} %bitcast.24.xr_ref.dyr_ref, bf16[512,512]{1,0:T(8,128)(2,1)} %fusion.place_ref.refs_2_, ...), custom_call_target="tpu_custom_call" | custom-call | flops 6000000000 | bytes 14000000 | tf_op jit(solution)/shard_map/state/pallas_call | solution.py:316
  158.4 1.8 collective-permute-start.1
  160.2 1.5 collective-permute-start.2
  163.7 13.2 %scan.3 = (bf16[256,8192]{1,0:T(8,128)(2,1)}, bf16[256,512]{1,0:T(8,128)(2,1)}, bf16[256,512]{1,0:T(8,128)(2,1)}, f32[2,256,128]{2,1,0:T(8,128)}) custom-call(bf16[256,4096]{1,0:T(8,128)(2,1)} %get-tuple-element.78.refs_0_, bf16[256,4096]{1,0:T(8,128)(2,1)} %get-tuple-element.79.refs_1_, ...), custom_call_target="tpu_custom_call", output_to_operand_aliasing={{0}: (14, {}), {1}: (15, {}), {2}: (16, {})} | custom-call | flops 8000000000 | bytes 10000000 | tf_op jit(solution)/shard_map/scan/pallas_call | solution.py:431
  176.9 2.0 finish.1
  178.9 1.3 fill_slot.1
  180.2 8.5 %all-to-all-done.2 = bf16[64,8,3072]{2,1,0:T(8,128)(2,1)S(1)} async-done(((bf16[64,8,3072]{2,1,0:T(8,128)(2,1)}), bf16[64,8,3072]{2,1,0:T(8,128)(2,1)S(1)}, u32[]{:S(2)}, u32[]{:S(2)}) %all-to-all-start.2) | async-done | bytes 3145760 | tf_op jit(solution)/shard_map/all_to_all | solution.py:136
  188.7 1.7 copy-done.1
  190.5 5.2 %all-to-all-start.3 = ((bf16[64,8,1152]{2,1,0:T(8,128)(2,1)}), bf16[64,8,1152]{2,1,0:T(8,128)(2,1)S(1)}, u32[]{:S(2)}, u32[]{:S(2)}) async-start(bf16[64,8,1152]{2,1,0:T(8,128)(2,1)} %bitcast.58), calls=%async_computation.3 | async-start | bytes 2359296 | tf_op jit(solution)/shard_map/all_to_all | solution.py:136
  195.7 8.3 %attention.3 = (bf16[256,4096]{1,0:T(8,128)(2,1)}, bf16[2,256,512]{2,1,0:T(8,128)(2,1)}, bf16[2,256,512]{2,1,0:T(8,128)(2,1)}) custom-call(bf16[512,3072]{1,0:T(8,128)(2,1)} %bitcast.66, bf16[512,3072]{1,0:T(8,128)(2,1)} %bitcast.67, bf16[512,512]{1,0:T(8,128)(2,1)} %fusion.place_ref.refs_2_, bf16[256,1024]{1,0:T(8,128)(2,1)} %get-tuple-element.90.refs_3_.refs_4_, ...), custom_call_target="tpu_custom_call" | custom-call | flops 12000000000 | bytes 8000000 | tf_op jit(solution)/shard_map/attention/pallas_call | solution.py:270
  204.0 5.3 %attention.4 = (bf16[256,4096]{1,0:T(8,128)(2,1)}, bf16[2,256,512]{2,1,0:T(8,128)(2,1)}, bf16[2,256,512]{2,1,0:T(8,128)(2,1)}) custom-call(bf16[512,3072]{1,0:T(8,128)(2,1)} %bitcast.68, bf16[512,3072]{1,0:T(8,128)(2,1)} %bitcast.69, bf16[512,512]{1,0:T(8,128)(2,1)} %fusion.place_ref.refs_2_, ...), custom_call_target="tpu_custom_call", output_to_operand_aliasing={{0}: (8, {}), {1}: (9, {}), {2}: (10, {})} | custom-call | flops 6000000000 | bytes 4000000 | tf_op jit(solution)/shard_map/attention/pallas_call | solution.py:270
  209.3 3.6 %all-to-all-done.3 = bf16[64,8,1152]{2,1,0:T(8,128)(2,1)S(1)} async-done(((bf16[64,8,1152]{2,1,0:T(8,128)(2,1)}), bf16[64,8,1152]{2,1,0:T(8,128)(2,1)S(1)}, u32[]{:S(2)}, u32[]{:S(2)}) %all-to-all-start.3) | async-done | bytes 1179680 | tf_op jit(solution)/shard_map/all_to_all | solution.py:136
  213.9 5.3 %attention.5 = (bf16[256,4096]{1,0:T(8,128)(2,1)}, bf16[2,256,512]{2,1,0:T(8,128)(2,1)}, bf16[2,256,512]{2,1,0:T(8,128)(2,1)}) custom-call(bf16[512,1152]{1,0:T(8,128)(2,1)} %bitcast.63, bf16[512,1152]{1,0:T(8,128)(2,1)} %bitcast.64, bf16[512,512]{1,0:T(8,128)(2,1)} %fusion.place_ref.refs_2_, ...), custom_call_target="tpu_custom_call", output_to_operand_aliasing={{0}: (8, {}), {1}: (9, {}), {2}: (10, {})} | custom-call | flops 6000000000 | bytes 4000000 | tf_op jit(solution)/shard_map/attention/pallas_call | solution.py:270
  219.1 5.6 %collective-permute-start.3 = (bf16[2,256,512]{2,1,0:T(8,128)(2,1)}, bf16[2,256,512]{2,1,0:T(8,128)(2,1)S(1)}, u32[]{:S(2)}, u32[]{:S(2)}) collective-permute-start(bf16[2,256,512]{2,1,0:T(8,128)(2,1)} %get-tuple-element.102), channel_id=1, source_target_pairs={{1,0},{3,2},{5,4},{7,6},{9,8},{11,10},{13,12},{15,14},{17,16},{19,... | collective-permute-start | bytes 1572872 | tf_op jit(solution)/shard_map/ppermute | solution.py:659
  224.7 1.5 sum_slots.1
  229.4 2.0 join.1
  (93 shorter events, 16.8 us)
Async XLA Ops:
  9.3 12.4 %copy-start.8 = (s32[64]{0:T(128)S(1)}, s32[64]{0:T(128)}, u32[]{:S(2)}) copy-start(s32[64]{0:T(128)} %constant.175.clone) | copy-start | bytes 772
  9.3 14.9 %copy-start.3 = (s32[64,64]{1,0:T(8,128)S(1)}, s32[64,64]{1,0:T(8,128)}, u32[]{:S(2)}) copy-start(s32[64,64]{1,0:T(8,128)} %param.25) | copy-start | bytes 49156
  9.4 76.0 %all-to-all-start = ((bf16[64,8,5248]{2,1,0:T(8,128)(2,1)}), bf16[64,8,5248]{2,1,0:T(8,128)(2,1)}, u32[]{:S(2)}, u32[]{:S(2)}) async-start(bf16[64,8,5248]{2,1,0:T(8,128)(2,1)} %bitcast.52), calls=%async_computation | async-start | bytes 10747904 | tf_op jit(solution)/shard_map/all_to_all | solution.py:136
  24.4 5.1 %copy-start.4 = (s32[1,512]{1,0:T(1,128)S(1)}, s32[1,512]{1,0:T(1,128)}, u32[]{:S(2)}) copy-start(s32[1,512]{1,0:T(1,128)} %param.24) | copy-start | bytes 6148
  29.5 7.6 %copy-start.6 = (s32[256]{0:T(256)}, s32[256]{0:T(256)S(1)}, u32[]{:S(2)}) copy-start(s32[256]{0:T(256)S(1)} %and_select_fusion) | copy-start | bytes 3076
  37.1 6.3 %slice-start = ((s32[256]{0:T(256)}), s32[128]{0:T(128)S(1)}, s32[]{:S(2)}) async-start(s32[256]{0:T(256)} %copy-done.6), calls=%async_computation.4 | async-start | bytes 1024 | tf_op jit(solution)/shard_map/slice | solution.py:607
  40.7 7.3 %copy-start.7 = (s32[256]{0:T(256)S(1)}, s32[256]{0:T(256)}, u32[]{:S(2)}) copy-start(s32[256]{0:T(256)} %copy-done.6) | copy-start | bytes 3076
  41.3 9.6 %copy-start.5 = (f32[8,288,128]{2,1,0:T(8,128)}, f32[8,288,128]{2,1,0:T(8,128)S(1)}, u32[]{:S(2)}) copy-start(f32[8,288,128]{2,1,0:T(8,128)S(1)} %select_dynamic-update-slice_fusion.refs_7_) | copy-start | bytes 3538948
  86.1 57.1 %all-to-all-start.1 = ((bf16[64,8,4096]{2,1,0:T(8,128)(2,1)}), bf16[64,8,4096]{2,1,0:T(8,128)(2,1)}, u32[]{:S(2)}, u32[]{:S(2)}) async-start(bf16[64,8,4096]{2,1,0:T(8,128)(2,1)} %bitcast.53), calls=%async_computation.1 | async-start | bytes 8388608 | tf_op jit(solution)/shard_map/all_to_all | solution.py:136
  105.5 4.6 %collective-permute-start = (bf16[128,4096]{1,0:T(8,128)(2,1)}, bf16[128,4096]{1,0:T(8,128)(2,1)S(1)}, u32[]{:S(2)}, u32[]{:S(2)}) collective-permute-start(bf16[128,4096]{1,0:T(8,128)(2,1)} %get-tuple-element.71), channel_id=1, source_target_pairs={{0,1},{1,0},{2,3},{3,2},{4,5},{5,4},{6,7},{7,6},{8,9},{9,8},{10,11... | collective-permute-start | bytes 3145736 | tf_op jit(solution)/shard_map/ppermute | solution.py:632
  110.1 1.0 copy-start.10
  143.2 45.6 %all-to-all-start.2 = ((bf16[64,8,3072]{2,1,0:T(8,128)(2,1)}), bf16[64,8,3072]{2,1,0:T(8,128)(2,1)S(1)}, u32[]{:S(2)}, u32[]{:S(2)}) async-start(bf16[64,8,3072]{2,1,0:T(8,128)(2,1)} %bitcast.27), calls=%async_computation.2 | async-start | bytes 6291456 | tf_op jit(solution)/shard_map/all_to_all | solution.py:136
  158.4 4.3 %collective-permute-start.1 = (bf16[128,4096]{1,0:T(8,128)(2,1)}, bf16[128,4096]{1,0:T(8,128)(2,1)S(1)}, u32[]{:S(2)}, u32[]{:S(2)}) collective-permute-start(bf16[128,4096]{1,0:T(8,128)(2,1)} %get-tuple-element.80), channel_id=1, source_target_pairs={{0,1},{1,0},{2,3},{3,2},{4,5},{5,4},{6,7},{7,6},{8,9},{9,8},{10,11... | collective-permute-start | bytes 3145736 | tf_op jit(solution)/shard_map/ppermute | solution.py:632
  160.2 35.4 %collective-permute-start.2 = (bf16[256,1024]{1,0:T(8,128)(2,1)}, bf16[256,1024]{1,0:T(8,128)(2,1)}, u32[]{:S(2)}, u32[]{:S(2)}) collective-permute-start(bf16[256,1024]{1,0:T(8,128)(2,1)} %get-tuple-element.90.refs_3_.refs_4_), channel_id=1, source_target_pairs={{0,1},{2,3},{4,5},{6,7},{8,9},{10,11},{12,13},{14,15},{16,17},{18,... | collective-permute-start | bytes 1572872 | tf_op jit(solution)/shard_map/ppermute | solution.py:628
  162.7 1.0 copy-start.9
  188.7 1.7 copy-start.1
  190.5 22.4 %all-to-all-start.3 = ((bf16[64,8,1152]{2,1,0:T(8,128)(2,1)}), bf16[64,8,1152]{2,1,0:T(8,128)(2,1)S(1)}, u32[]{:S(2)}, u32[]{:S(2)}) async-start(bf16[64,8,1152]{2,1,0:T(8,128)(2,1)} %bitcast.58), calls=%async_computation.3 | async-start | bytes 2359296 | tf_op jit(solution)/shard_map/all_to_all | solution.py:136
  212.8 1.0 copy-start
  219.1 9.5 %collective-permute-start.3 = (bf16[2,256,512]{2,1,0:T(8,128)(2,1)}, bf16[2,256,512]{2,1,0:T(8,128)(2,1)S(1)}, u32[]{:S(2)}, u32[]{:S(2)}) collective-permute-start(bf16[2,256,512]{2,1,0:T(8,128)(2,1)} %get-tuple-element.102), channel_id=1, source_target_pairs={{1,0},{3,2},{5,4},{7,6},{9,8},{11,10},{13,12},{15,14},{17,16},{19,... | collective-permute-start | bytes 1572872 | tf_op jit(solution)/shard_map/ppermute | solution.py:659
  226.2 1.3 collective-permute-start.4
  228.6 0.8 copy-start.2
